TPU v7x, 256 devices: a whole 4x4x8 slice. The times are simulated.
256 devices in a mesh: section: 16 (over z, core), tensor: 4 (over y), dp: 4 (over x).
Axes of the slice: x: 4, y: 4, z: 8, core: 2. Of those that a mesh axis runs over, the one named last changes fastest.
Arguments:
- updates: bfloat16 [16, 64, 8192], P('section', 'dp', 'tensor')
- norm_gain: bfloat16 [8192], replicated, may hold values from 0.25 to 1.75
- head: bfloat16 [8192, 32000], P(None, ('section', 'tensor'))
- targets: int32 [64], P('dp'), may hold values from 0 to 31999
- curriculum: int32 [16], replicated, may hold values from 1 to 16
Outputs:
- update_grad: float32 [16, 64, 8192], P('section', 'dp', 'tensor')
- head_grad: bfloat16 [8192, 32000], P('dp', ('section', 'tensor'))
- section_losses: float32 [16], replicated
Inputs may be any that keep to these rules, and one draw needn't show every extreme that they name: `curriculum`: numerators over a fixed denominator of 4.
All inputs are finite; a program needn't handle non-finite values.
Results may differ from a plain program's by a relative error of at most 0.013.
Values may be sent and summed in bfloat16 or wider, within the bound.
A program may use at most 128 MiB of HBM per device.

v0:
```python
import jax
import jax.numpy as jnp
from jax import lax
from jax.experimental import pallas as pl
from jax.experimental.pallas import tpu as pltpu
from jax.sharding import PartitionSpec as P

F32 = jnp.float32
BF16 = jnp.bfloat16
epsilon = 1e-05
scale_denominator = 4.0

NY = 4
NX = 4
NZ = 8

GATHER_Y = (0, -1, 1, 2)
SCATTER_Y = (2, 1, -1, 0)
SCATTER_Z = (4, 3, -3, 2, -2, 1, -1, 0)


def wrap(value, count):
    return lax.rem(value + 2 * count, count)


CODE_TOP = 32766.0


def encode(value):
    root = value * lax.rsqrt(jnp.maximum(jnp.abs(value), 1e-12))
    return jnp.round(root).astype(jnp.int32).astype(jnp.int16)


def decode(code):
    root = code.astype(jnp.int32).astype(F32)
    return root * jnp.abs(root)


def kernel(
    upd, gain, head, targets, curriculum,
    upd_grad, head_grad, losses,
    U, HEAD, H, HM, R, PB, QS, SB, QR, RB, RX, GX, GN, L, GAIN, SQ, INV, COEF, BND, SC, HG, ST1, ST2, CT1, CT2, NL,
    local_sem, r_own, r_sib, s_sib, s_p, s_m, s_y,
    s_st, r_st1, r_st2, s_ct, r_ct1, r_ct2, s_nl, r_nl, s_hg,
    s_rx, r_rx, s_rxs, r_rxs, s_g, r_g, s_sb, r_sb, s_rs, r_rs,
):
    tok, q = upd.shape[1], upd.shape[2]
    width = q * NY
    vdev = head.shape[0]
    vpad = L.shape[0]
    half = NZ * tok
    rows = 2 * half
    s = lax.axis_index("section")
    y = lax.axis_index("tensor")
    x = lax.axis_index("dp")
    core = lax.rem(s, 2)
    z = lax.div(s, 2)
    sibling = s + 1 - 2 * core

    def copy_to(src, dst, ssem, rsem, **device):
        return pltpu.make_async_remote_copy(
            src_ref=src, dst_ref=dst, send_sem=ssem, recv_sem=rsem,
            device_id=device, device_id_type=pl.DeviceIdType.MESH,
        )

    def arrived(dst, rsem):
        copy_to(dst, dst, local_sem.at[0], rsem, section=sibling).wait_recv()

    def at_z(zz):
        return 2 * wrap(zz, NZ) + core

    def block_rows(cc, zz):
        return pl.ds(pl.multiple_of((cc * NZ + zz) * tok, tok), tok)

    def slice_y(yy):
        return pl.ds(pl.multiple_of(yy * q, q), q)

    def half_rows(cc):
        return pl.ds(pl.multiple_of(cc * half, half), half)

    barrier = pltpu.get_barrier_semaphore()
    peers = [dict(section=sibling)]
    peers += [dict(tensor=wrap(y + d, NY)) for d in range(1, NY)]
    peers += [dict(section=sibling, tensor=wrap(y + d, NY)) for d in range(1, NY)]
    peers += [dict(section=at_z(z + d)) for d in range(1, NZ)]
    peers += [dict(dp=wrap(x + d, NX)) for d in range(1, NX)]
    for peer in peers:
        pl.semaphore_signal(barrier, inc=1, device_id=peer, device_id_type=pl.DeviceIdType.MESH)
    load_head = pltpu.make_async_copy(head, HEAD, local_sem.at[1])
    load_head.start()
    pl.semaphore_wait(barrier, len(peers))

    own = upd.at[0]

    def ublk(cc, zz, yy):
        return U.at[block_rows(cc, zz), slice_y(yy)]

    keep_own = pltpu.make_async_copy(own, ublk(core, z, y), local_sem.at[2])
    keep_own.start()

    whole = vdev // 16 * 16

    def pad_head(n):
        cols = slice(n * (width // 8), (n + 1) * (width // 8))
        block = HEAD[0:whole, cols]
        H[0:whole, cols] = block
        H[whole:vpad, cols] = jnp.zeros((vpad - whole, width // 8), BF16)
        tail = HEAD[whole:vdev, cols]
        H[whole:vdev, cols] = tail
        HM[n:n + 1, :] = jnp.maximum(
            jnp.max(jnp.abs(block).astype(F32), axis=0, keepdims=True),
            jnp.max(jnp.abs(tail).astype(F32), axis=0, keepdims=True),
        )

    @pl.when(core == 0)
    def _():
        copies = []

        def send(src, dst, ssem, rsem, **device):
            copies.append(copy_to(src, dst, ssem, rsem, **device))
            copies[-1].start()

        def to_sibling(src, zz, yy):
            send(src, ublk(0, zz, yy), s_sib.at[zz, yy], r_sib.at[zz, yy], section=sibling)

        def pass_on(src, zz, yy, k, j, side):
            dst, rsem = ublk(0, zz, yy), r_own.at[zz, yy]
            near = k + 1 < NZ // 2
            last = k + 1 == NZ // 2
            if side != "right" and (near or (last and j < NY // 2)):
                send(src, dst, s_p.at[k, j], rsem, section=at_z(z + 1))
            if side != "left" and (near or (last and j >= NY // 2)):
                send(src, dst, s_m.at[k, j], rsem, section=at_z(z - 1))
            to_sibling(src, zz, yy)

        for n, d in enumerate((2, 1, -1)):
            send(own, ublk(0, z, y), s_y.at[n, 0], r_own.at[z, y], tensor=wrap(y + d, NY))
        pass_on(own, z, y, 0, 0, "here")
        for j in range(1, NY):
            yy = wrap(y + GATHER_Y[j], NY)
            arrived(ublk(0, z, yy), r_own.at[z, yy])
            pass_on(ublk(0, z, yy), z, yy, 0, j, "here")
        load_head.wait()
        for k in range(1, NZ // 2 + 1):
            for j in range(NY):
                yy = wrap(y + GATHER_Y[j], NY)
                for side, d in (("left", -k), ("right", k)):
                    if k == NZ // 2 and (j < NY // 2) != (side == "left"):
                        continue
                    zz = wrap(z + d, NZ)
                    arrived(ublk(0, zz, yy), r_own.at[zz, yy])
                    pass_on(ublk(0, zz, yy), zz, yy, k, j, side)
                if k < 3:
                    pad_head((k - 1) * NY + j)
        for copy in copies:
            copy.wait_send()

    @pl.when(core == 1)
    def _():
        copies = []
        order = (0, -1, 1, -2, 2, -3, 3, -4)

        def send(src, dst, ssem, rsem, **device):
            copies.append(copy_to(src, dst, ssem, rsem, **device))
            copies[-1].start()

        for n, d in enumerate(order):
            zz = wrap(z + d, NZ)
            dst = ublk(1, zz, y)
            src = own if n == 0 else dst
            if n > 0:
                arrived(dst, r_own.at[zz, y])
            if d in (0, -2):
                send(src, dst, s_p.at[-d, 0], r_own.at[zz, y], section=at_z(z + 1))
                send(src, dst, s_p.at[-d, 1], r_own.at[zz, y], section=at_z(z + 2))
            if d in (0, 2):
                send(src, dst, s_m.at[d, 0], r_own.at[zz, y], section=at_z(z - 1))
            if d == 0:
                send(src, dst, s_m.at[d, 1], r_own.at[zz, y], section=at_z(z - 2))
            for m, step in enumerate((1, -1, 2)):
                send(src, dst, s_y.at[m, n], r_own.at[zz, y], tensor=wrap(y + step, NY))
            send(src, dst, s_sib.at[zz, y], r_sib.at[zz, y], section=sibling)
        load_head.wait()
        for n, d in enumerate(order):
            zz = wrap(z + d, NZ)
            for step in (-1, 1, 2):
                yy = wrap(y + step, NY)
                dst = ublk(1, zz, yy)
                arrived(dst, r_own.at[zz, yy])
                send(dst, dst, s_sib.at[zz, yy], r_sib.at[zz, yy], section=sibling)
            pad_head(n)
        for copy in copies:
            copy.wait_send()

    head_top = jnp.max(jnp.max(HM[...], axis=0, keepdims=True), axis=1, keepdims=True)

    def wait_sibling(n, carry):
        zz, yy = lax.div(n, NY), lax.rem(n, NY)
        arrived(ublk(1 - core, zz, yy), r_sib.at[zz, yy])
        return carry

    lax.fori_loop(0, NZ * NY, wait_sibling, 0)
    keep_own.wait()

    chunk = 512
    groups = chunk // 128

    def section_rows(k):
        return pl.ds(((k % 2) * NZ + k // 2) * tok, tok)

    SQ[...] = jnp.zeros_like(SQ)

    def squares(f, carry):
        cols = pl.ds(pl.multiple_of(f * chunk, chunk), chunk)
        hidden = jnp.zeros((tok, chunk), F32)
        for k in range(2 * NZ):
            hidden = hidden + U[section_rows(k), cols].astype(F32)
            square = hidden * hidden
            part = square[:, :128]
            for g in range(1, groups):
                part = part + square[:, g * 128:(g + 1) * 128]
            SQ[section_rows(k), :] += part
        return carry

    def gain_row(f, count):
        return jnp.concatenate([GAIN[pl.ds(f * count + g, 1), :] for g in range(count)], axis=1)

    GAIN[...] = gain[...].astype(F32)
    lax.fori_loop(0, width // chunk, squares, 0)
    mean = jnp.sum(SQ[...], axis=1, keepdims=True) / width
    INV[...] = jnp.broadcast_to(lax.rsqrt(mean + epsilon), (rows, 128))

    def normalize(f, carry):
        cols = pl.ds(pl.multiple_of(f * chunk, chunk), chunk)
        scale = gain_row(f, groups)
        hidden = jnp.zeros((tok, chunk), F32)
        for k in range(2 * NZ):
            hidden = hidden + U[section_rows(k), cols].astype(F32)
            inverse = INV[section_rows(k), :]
            R[section_rows(k), cols] = (
                scale * hidden * jnp.concatenate([inverse] * groups, axis=1)
            ).astype(BF16)
        return carry

    lax.fori_loop(0, width // chunk, normalize, 0)

    part = width // NX

    def slice_x(xx):
        return pl.ds(pl.multiple_of(xx * part, part), part)

    def rx_rows(xx, cc):
        return pl.ds(pl.multiple_of(xx * rows + cc * half, half), half)

    def x_rows(xx):
        return pl.ds(pl.multiple_of(xx * rows, rows), rows)

    row_copies = []
    for n, d in enumerate((1, -1, 2)):
        xx = wrap(x + d, NX)
        row_copies.append(copy_to(
            R.at[half_rows(core), slice_x(xx)], RX.at[rx_rows(x, core), :],
            s_rx.at[n], r_rx.at[x], dp=xx,
        ))
        row_copies[-1].start()
    keep_rows = pltpu.make_async_copy(R.at[:, slice_x(x)], RX.at[x_rows(x), :], local_sem.at[3])
    keep_rows.start()

    depth = 4096
    pad = lax.broadcasted_iota(jnp.int32, (vpad, rows), 0) >= vdev
    L[...] = jnp.where(pad, -1e30, 0.0)

    def logits_step(f, carry):
        cols = pl.ds(pl.multiple_of(f * depth, depth), depth)
        L[...] += lax.dot_general(
            H[:, cols], R[:, cols], (((1,), (1,)), ((), ())), preferred_element_type=F32
        )
        return carry

    lax.fori_loop(0, width // depth, logits_step, 0)

    first = (s * NY + y) * vdev
    column = lax.broadcasted_iota(jnp.int32, (1, rows), 1)
    token = lax.rem(column, tok)
    block = lax.div(column, tok)
    wanted = jnp.zeros((1, rows), jnp.int32)
    for i in range(tok):
        wanted = jnp.where(token == i, targets[i], wanted)
    numerator = jnp.zeros((1, rows), jnp.int32)
    for b in range(2 * NZ):
        numerator = jnp.where(block == b, curriculum[(b % NZ) * 2 + b // NZ], numerator)
    weight = numerator.astype(F32) / scale_denominator
    hit = lax.broadcasted_iota(jnp.int32, (vpad, rows), 0) + first == wanted
    hit = jnp.logical_and(hit, jnp.logical_not(pad))
    logits = L[...]
    top = jnp.max(logits, axis=0, keepdims=True)
    total = jnp.sum(jnp.exp(logits - top), axis=0, keepdims=True)
    target = jnp.sum(jnp.where(hit, logits, 0.0), axis=0, keepdims=True)
    here = core * NY + y
    ST1[here] = jnp.concatenate(
        [top, total, target, jnp.broadcast_to(head_top, (1, rows)), jnp.zeros((4, rows), F32)], axis=0
    )

    def combine(parts):
        top = parts[0][0:1]
        for p in parts[1:]:
            top = jnp.maximum(top, p[0:1])
        total = parts[0][1:2] * jnp.exp(parts[0][0:1] - top)
        target = parts[0][2:3]
        largest = parts[0][3:4]
        for p in parts[1:]:
            largest = jnp.maximum(largest, p[3:4])
            total = total + p[1:2] * jnp.exp(p[0:1] - top)
            target = target + p[2:3]
        return jnp.concatenate([top, total, target, largest, jnp.zeros((4, rows), F32)], axis=0)

    def add_up(parts):
        total = parts[0]
        for p in parts[1:]:
            total = total + p
        return total

    def exchange(level, B1, B2, ssem, r1, r2):
        if level == 1:
            out = [copy_to(B1.at[here], B1.at[here], ssem.at[0], r1.at[here], section=sibling)]
            for n, d in enumerate((1, 3, 2)):
                yy = wrap(y + d, NY)
                out.append(copy_to(B1.at[here], B1.at[here], ssem.at[n + 1], r1.at[here], tensor=yy))
                out.append(copy_to(
                    B1.at[here], B1.at[here], ssem.at[n + NY], r1.at[here], section=sibling, tensor=yy
                ))
        else:
            out = [
                copy_to(B2.at[z], B2.at[z], ssem.at[n + 2 * NY], r2.at[z], section=at_z(z + d))
                for n, d in enumerate((4, 3, 5, 2, 6, 1, 7))
            ]
        for copy in out:
            copy.start()
        return out

    def collect(level, B1, B2, r1, r2):
        if level == 1:
            for cc, d in ((1, 0), (0, 1), (0, 3), (1, 1), (1, 3), (0, 2), (1, 2)):
                slot = lax.rem(core + cc, 2) * NY + wrap(y + d, NY)
                arrived(B1.at[slot], r1.at[slot])
            return [B1[k] for k in range(2 * NY)]
        for d in (1, 7, 2, 6, 3, 5, 4):
            arrived(B2.at[wrap(z + d, NZ)], r2.at[wrap(z + d, NZ)])
        return [B2[k] for k in range(NZ)]

    small = []
    stat_bufs, stat_sems = (ST1, ST2), (r_st1, r_st2)
    small += exchange(1, *stat_bufs, s_st, *stat_sems)
    ST2[z] = combine(collect(1, *stat_bufs, *stat_sems))
    small += exchange(2, *stat_bufs, s_st, *stat_sems)
    final = combine(collect(2, *stat_bufs, *stat_sems))
    lse_row = final[0:1] + jnp.log(final[1:2])
    NL[x] = jnp.broadcast_to(lse_row - final[2:3], (8, rows))
    for n, d in enumerate((1, 2, 3)):
        small.append(copy_to(NL.at[x], NL.at[x], s_nl.at[n], r_nl.at[x], dp=wrap(x + d, NX)))
        small[-1].start()

    logits = L[...]
    probs = jnp.exp(logits - lse_row)
    grad = weight * (probs - jnp.where(hit, 1.0, 0.0))
    rounded = grad.astype(BF16)
    GX[x] = rounded
    GN[...] = jnp.transpose(rounded)
    product = jnp.sum(rounded.astype(F32) * logits, axis=0, keepdims=True)
    CT1[here] = jnp.broadcast_to(product, (8, rows))
    inner_bufs, inner_sems = (CT1, CT2), (r_ct1, r_ct2)
    small += exchange(1, *inner_bufs, s_ct, *inner_sems)
    for n, d in enumerate((1, -1, 2)):
        row_copies.append(copy_to(
            GX.at[x], GX.at[x], s_g.at[n], r_g.at[x], dp=wrap(x + d, NX)
        ))
        row_copies[-1].start()

    later = jnp.zeros((tok, 128), F32)
    for k in reversed(range(2 * NZ)):
        later = later + INV[section_rows(k), :] * (curriculum[k].astype(F32) / scale_denominator)
        bound = jnp.maximum(later * (final[3:4, 0:128] * 2.03), 1e-20)
        BND[section_rows(k), :] = bound
        SC[section_rows(k), :] = (CODE_TOP * CODE_TOP) / bound

    def pair_sum(cc, zz, yy):
        return PB[block_rows(cc, zz), slice_y(yy)] + decode(
            SB[pl.ds(pl.multiple_of(zz * tok, tok), tok), slice_y(yy)]
        )

    def start_coded(value, slot, **device):
        QR[slot] = encode(value)
        copy = copy_to(QR.at[slot], RB.at[slot], s_rs.at[slot], r_rs.at[slot], **device)
        copy.start()
        return copy

    def received(slot):
        arrived(RB.at[slot], r_rs.at[slot])
        return decode(RB[slot])

    def slice_of(j):
        return wrap(y + SCATTER_Y[j], NY)

    up3, down3, far4, up1, down1, up2, down2, over_y = range(0, 8 * NY, NY)
    count = len(SCATTER_Z)
    fourth, third, second, next_up, third_down, second_down, next_down = range(3 * count, 3 * count + 7)

    def first_even(j):
        yy = slice_of(j)
        arrived(SB.at[:, slice_y(yy)], r_sb.at[j])
        way = 2 if j < NY // 2 else -2
        start_coded(pair_sum(0, wrap(z + 4, NZ), yy), far4 + j, section=at_z(z + way))
        start_coded(pair_sum(0, wrap(z + 3, NZ), yy), up3 + j, section=at_z(z + 1))
        start_coded(pair_sum(0, wrap(z - 3, NZ), yy), down3 + j, section=at_z(z - 1))
        start_coded(pair_sum(0, wrap(z + 1, NZ), yy), up1 + j, section=at_z(z + 1))
        start_coded(pair_sum(0, wrap(z - 1, NZ), yy), down1 + j, section=at_z(z - 1))

    def first_odd(j):
        yy = slice_of(j)
        arrived(SB.at[:, slice_y(yy)], r_sb.at[j])
        for n in range(count):
            start_coded(pair_sum(1, wrap(z + SCATTER_Z[n], NZ), yy), j * count + n, tensor=yy)

    def first_step(j):
        pl.when(core == 0)(lambda: first_even(j))
        pl.when(core == 1)(lambda: first_odd(j))

    def sent(slot):
        copy_to(QR.at[slot], RB.at[slot], s_rs.at[slot], r_rs.at[slot], section=sibling).wait_send()

    sib_copies = []
    wide = 1024
    for j in range(NY):
        yy = wrap(y + SCATTER_Y[j], NY)

        def share(f, carry):
            cols = pl.ds(pl.multiple_of(yy * q + f * wide, wide), wide)
            term = jnp.dot(GN[...], H[:, cols], preferred_element_type=F32)
            later = jnp.zeros((tok, wide), F32)
            for k in reversed(range(2 * NZ)):
                at = ((k % 2) * NZ + k // 2) * tok
                inverse = INV[section_rows(k), :]
                later = later + term[at:at + tok] * jnp.concatenate([inverse] * (wide // 128), axis=1)
                PB[section_rows(k), cols] = later * jnp.concatenate([SC[section_rows(k), :]] * (wide // 128), axis=1)
            QS[:, cols] = encode(PB[half_rows(1 - core), cols])
            return carry

        lax.fori_loop(0, q // wide, share, 0)
        sib_copies.append(copy_to(
            QS.at[:, slice_y(yy)], SB.at[:, slice_y(yy)],
            s_sb.at[j], r_sb.at[j], section=sibling,
        ))
        sib_copies[-1].start()
        if j > 0:
            first_step(j - 1)
        if j == 1:
            CT2[z] = add_up(collect(1, *inner_bufs, *inner_sems))
            small += exchange(2, *inner_bufs, s_ct, *inner_sems)

    projected = add_up(collect(2, *inner_bufs, *inner_sems))[0:1]
    projected = jnp.transpose(jnp.broadcast_to(projected, (128, rows)))
    COEF[...] = INV[...] * INV[...] * projected / width

    def second_term(f, carry):
        cols = pl.ds(pl.multiple_of(y * q + f * chunk, chunk), chunk)
        hidden = jnp.zeros((tok, chunk), F32)
        later = jnp.zeros((tok, chunk), F32)
        for k in range(2 * NZ):
            hidden = hidden + U[section_rows(k), cols].astype(F32)
            factor = jnp.where(k >= s, COEF[section_rows(k), :], 0.0)
            later = later + hidden * jnp.concatenate([factor] * groups, axis=1)
        upd_grad[0, :, pl.ds(pl.multiple_of(f * chunk, chunk), chunk)] = later
        return carry

    lax.fori_loop(0, q // chunk, second_term, 0)
    own_gain = gain_row(y, q // 128)

    def pass_rows(copies, d):
        xx = wrap(x + d, NX)
        dst = RX.at[rx_rows(xx, core), :]
        arrived(dst, r_rx.at[xx])
        copies.append(copy_to(dst, dst, s_rxs.at[xx], r_rxs.at[xx], section=sibling))
        copies[-1].start()

    def rows_here():
        for d in (1, -1, 2):
            xx = wrap(x + d, NX)
            arrived(GX.at[xx], r_g.at[xx])
            arrived(RX.at[rx_rows(xx, 1 - core), :], r_rxs.at[xx])

    piece = part // (2 * NX)

    def head_part(f):
        cols = slice(f * piece, (f + 1) * piece)
        total = jnp.zeros((vpad, piece), F32)
        for k in range(NX):
            total = total + jnp.dot(GX[k], RX[k * rows:(k + 1) * rows, cols], preferred_element_type=F32)
        HG[:, cols] = total[0:vdev].astype(BF16)
        out = pltpu.make_async_copy(HG.at[:, cols], head_grad.at[:, cols], s_hg.at[f])
        out.start()
        return out

    keep_rows.wait()

    def write_update(total):
        back = BND[block_rows(core, z), :] / (CODE_TOP * CODE_TOP)
        total = total * jnp.concatenate([back] * (q // 128), axis=1)
        upd_grad[0] = own_gain * total - upd_grad[0]

    @pl.when(core == 0)
    def _():
        copies, outs = [], []

        def second_even(j):
            yy = slice_of(j)
            total = pair_sum(0, wrap(z + 2, NZ), yy) + received(up3 + j)
            if j < NY // 2:
                total = total + received(far4 + j)
            start_coded(total, up2 + j, section=at_z(z + 2))
            total = pair_sum(0, wrap(z - 2, NZ), yy) + received(down3 + j)
            if j >= NY // 2:
                total = total + received(far4 + j)
            start_coded(total, down2 + j, section=at_z(z - 2))

        second_even(0)
        first_even(NY - 1)
        pass_rows(copies, 1)
        pass_rows(copies, -1)
        for j in range(1, NY):
            second_even(j)
        pass_rows(copies, 2)
        for j in range(NY):
            total = pair_sum(0, z, slice_of(j))
            for slot in (up1, down1, up2, down2):
                total = total + received(slot + j)
            if j < NY - 1:
                start_coded(total, over_y + j, tensor=slice_of(j))
        rows_here()
        for n in range(2 * NX):
            outs.append(head_part(n))
        for j in (1, 2, 0):
            total = total + received(over_y + j)
        write_update(total)
        for slot in range(over_y + NY - 1):
            sent(slot)
        for copy in copies:
            copy.wait_send()
        for copy in outs:
            copy.wait()

    @pl.when(core == 1)
    def _():
        copies, outs = [], []
        pass_rows(copies, 1)
        pass_rows(copies, -1)
        arrived(SB.at[:, slice_y(y)], r_sb.at[NY - 1])
        for n, o in enumerate(SCATTER_Z):
            total = pair_sum(1, wrap(z + o, NZ), y)
            for j in range(NY - 1):
                total = total + received(j * count + n)
            if o == 4:
                start_coded(total, fourth, section=at_z(z + 2))
            elif o == 3:
                start_coded(total, third, section=at_z(z + 1))
            elif o == -3:
                start_coded(total, third_down, section=at_z(z - 1))
            elif o == 2:
                start_coded(total + received(fourth) + received(third), second, section=at_z(z + 2))
            elif o == -2:
                start_coded(total + received(third_down), second_down, section=at_z(z - 2))
            elif o == 1:
                start_coded(total, next_up, section=at_z(z + 1))
            elif o == -1:
                start_coded(total, next_down, section=at_z(z - 1))
            if o == -2:
                pass_rows(copies, 2)
        rows_here()
        for n in range(2 * NX):
            outs.append(head_part(n))
        for slot in (next_up, next_down, second, second_down):
            total = total + received(slot)
        write_update(total)
        for slot in range(next_down + 1):
            sent(slot)
        for copy in copies:
            copy.wait_send()
        for copy in outs:
            copy.wait()

    for d in (1, -1, 2):
        xx = wrap(x + d, NX)
        arrived(NL.at[xx], r_nl.at[xx])
    nll = add_up([NL[k] for k in range(NX)])
    nll = jnp.transpose(jnp.broadcast_to(nll[0:1], (128, rows)))
    means = [None] * (2 * NZ)
    for b in range(2 * NZ):
        means[(b % NZ) * 2 + b // NZ] = jnp.sum(
            nll[b * tok:(b + 1) * tok], axis=0, keepdims=True
        ) / (tok * NX)
    means.append(jnp.zeros((128 - 2 * NZ, 128), F32))
    losses[...] = jnp.transpose(jnp.concatenate(means, axis=0))[0:8]

    for copy in row_copies + sib_copies + small:
        copy.wait_send()


def hand_over(upd_in, head_in, losses_in, upd_out, head_out, losses_out, upd_held, head_held, sem):
    count = 4
    step = head_in.shape[1] // count
    pairs = [(upd_in, upd_held, upd_out)]
    for n in range(count):
        cols = pl.ds(n * step, step)
        pairs.append((head_in.at[:, cols], head_held.at[:, cols], head_out.at[:, cols]))
    reads = [pltpu.make_async_copy(a, b, sem.at[0, n]) for n, (a, b, _) in enumerate(pairs)]
    writes = [pltpu.make_async_copy(b, c, sem.at[1, n]) for n, (_, b, c) in enumerate(pairs)]
    for copy in reads:
        copy.start()
    losses_out[...] = losses_in[0:1, 0:2 * NZ]
    for read, write in zip(reads, writes):
        read.wait()
        write.start()
    for copy in writes:
        copy.wait()


def body(updates, norm_gain, head, targets, curriculum):
    _, tok, q = updates.shape
    width, vdev = head.shape
    vpad = (vdev + 15) // 16 * 16
    rows = 2 * NZ * tok
    vmem = pl.BlockSpec(memory_space=pltpu.VMEM)
    smem = pl.BlockSpec(memory_space=pltpu.SMEM)
    hbm = pl.BlockSpec(memory_space=pl.ANY)
    dma = lambda *shape: pltpu.SemaphoreType.DMA(shape)
    slots = NZ * NY + NY
    upd_grad, head_grad, losses = pl.pallas_call(
        kernel,
        out_shape=(
            jax.ShapeDtypeStruct((1, tok, q), F32),
            jax.ShapeDtypeStruct((vdev, width // NX), BF16),
            jax.ShapeDtypeStruct((8, 128), F32),
        ),
        in_specs=[vmem, vmem, hbm, smem, smem],
        out_specs=(vmem, hbm, vmem),
        scratch_shapes=[
            pltpu.VMEM((rows, width), BF16),
            pltpu.VMEM((vdev, width), BF16),
            pltpu.VMEM((vpad, width), BF16),
            pltpu.VMEM((8, width // 8), F32),
            pltpu.VMEM((rows, width), BF16),
            pltpu.VMEM((rows, width), F32),
            pltpu.VMEM((rows // 2, width), jnp.int16),
            pltpu.VMEM((rows // 2, width), jnp.int16),
            pltpu.VMEM((slots, tok, q), jnp.int16),
            pltpu.VMEM((slots, tok, q), jnp.int16),
            pltpu.VMEM((NX * rows, width // NX), BF16),
            pltpu.VMEM((NX, vpad, rows), BF16),
            pltpu.VMEM((rows, vpad), BF16),
            pltpu.VMEM((vpad, rows), F32),
            pltpu.VMEM((width // 128, 128), F32),
            pltpu.VMEM((rows, 128), F32),
            pltpu.VMEM((rows, 128), F32),
            pltpu.VMEM((rows, 128), F32),
            pltpu.VMEM((rows, 128), F32),
            pltpu.VMEM((rows, 128), F32),
            pltpu.VMEM((vdev, width // NX), BF16),
            pltpu.VMEM((2 * NY, 8, rows), F32),
            pltpu.VMEM((NZ, 8, rows), F32),
            pltpu.VMEM((2 * NY, 8, rows), F32),
            pltpu.VMEM((NZ, 8, rows), F32),
            pltpu.VMEM((NX, 8, rows), F32),
            dma(4), dma(NZ, NY), dma(NZ, NY), dma(NZ, NY), dma(NZ, NY), dma(NZ, NY), dma(3, NZ),
            dma(2 * NY + NZ), dma(2 * NY), dma(NZ), dma(2 * NY + NZ), dma(2 * NY), dma(NZ), dma(NX), dma(NX), dma(NX * 2),
            dma(NX), dma(NX), dma(NX), dma(NX), dma(NX), dma(NX), dma(NY), dma(NY), dma(slots), dma(slots),
        ],
        compiler_params=pltpu.CompilerParams(
            collective_id=0, has_side_effects=True, vmem_limit_bytes=60 * 1024 * 1024
        ),
    )(updates, norm_gain.reshape(width // 128, 128), head.T, targets, curriculum)
    upd_grad, head_grad, losses = pl.pallas_call(
        hand_over,
        out_shape=(
            jax.ShapeDtypeStruct(upd_grad.shape, F32),
            jax.ShapeDtypeStruct(head_grad.shape, BF16),
            jax.ShapeDtypeStruct((1, 2 * NZ), F32),
        ),
        in_specs=[hbm, hbm, vmem],
        out_specs=(hbm, hbm, vmem),
        scratch_shapes=[pltpu.VMEM(upd_grad.shape, F32), pltpu.VMEM(head_grad.shape, BF16), dma(2, 5)],
        compiler_params=pltpu.CompilerParams(vmem_limit_bytes=60 * 1024 * 1024),
    )(upd_grad, head_grad, losses)
    return upd_grad, head_grad.T, losses.reshape(2 * NZ)


def solution(mesh):
    return jax.shard_map(
        body,
        mesh=mesh,
        in_specs=(P("section", "dp", "tensor"), P(), P(None, ("section", "tensor")), P("dp"), P()),
        out_specs=(P("section", "dp", "tensor"), P("dp", ("section", "tensor")), P()),
        check_vma=False,
    )
```

profile of v0, /device:TPU:1, one launch (start us, length us, event | category | flops | bytes accessed | tf_op | source)
XLA Modules:
  0.0 85.3 jit_solution(9972833034904433111)
XLA Ops:
  0.6 80.8 %shard_map.76 = (f32[1,16,2048]{2,1,0:T(8,128)}, bf16[500,2048]{1,0:T(8,128)(2,1)}, f32[8,128]{1,0:T(8,128)}) custom-call(bf16[1,16,2048]{2,1,0:T(8,128)(2,1)} %upd.1, bf16[64,128]{1,0:T(8,128)(2,1)} %bitcast.5, bf16[500,8192]{1,0:T(8,128)(2,1)} %bitcast.4, s32[16]{0:T(128)} %targets.1, s32[16]{0:T(128)} %curriculum.1), custom_call_target="tpu_custom_call" | custom-call | tf_op jit(solution)/shard_map/pallas_call | solution.py:636
  81.4 3.7 %shard_map.77 = (f32[1,16,2048]{2,1,0:T(8,128)}, bf16[500,2048]{1,0:T(8,128)(2,1)}, f32[1,16]{1,0:T(1,128)}) custom-call(f32[1,16,2048]{2,1,0:T(8,128)} %get-tuple-element.9.upd_in, bf16[500,2048]{1,0:T(8,128)(2,1)} %get-tuple-element.10.head_in, f32[8,128]{1,0:T(8,128)} %get-tuple-element.11.losses_in), custom_call_target="tpu_custom_call" | custom-call | tf_op jit(solution)/shard_map/pallas_call | solution.py:680
where the time goes:
time: 85.5 us; the launch traced here: 85.3 us
  Pallas kernels  84.5 us (99%)
    pallas_call x1, Pallas kernels, body(): pl.pallas_call(kernel, out_shape=(jax.ShapeDtypeStruct((1, tok, q), F32),...  80.8 us
    pallas_call x1, Pallas kernels, body(): pl.pallas_call(hand_over, out_shape=(jax.ShapeDtypeStruct(upd_grad.shape,...  3.69 us

commit v1 on v0

--- a/solution.py
+++ b/solution.py
@@ -39,7 +39,7 @@
 def kernel(
     upd, gain, head, targets, curriculum,
     upd_grad, head_grad, losses,
-    U, HEAD, H, HM, R, PB, QS, SB, QR, RB, RX, GX, GN, L, GAIN, SQ, INV, COEF, BND, SC, HG, ST1, ST2, CT1, CT2, NL,
+    U, HEAD, H, HM, R, PB, QS, SB, QR, RB, RX, GX, GN, L, GAIN16, GAIN, SQ, INV, COEF, BND, SC, HG, ST1, ST2, CT1, CT2, NL,
     local_sem, r_own, r_sib, s_sib, s_p, s_m, s_y,
     s_st, r_st1, r_st2, s_ct, r_ct1, r_ct2, s_nl, r_nl, s_hg,
     s_rx, r_rx, s_rxs, r_rxs, s_g, r_g, s_sb, r_sb, s_rs, r_rs,
@@ -87,16 +87,18 @@
     for peer in peers:
         pl.semaphore_signal(barrier, inc=1, device_id=peer, device_id_type=pl.DeviceIdType.MESH)
     load_head = pltpu.make_async_copy(head, HEAD, local_sem.at[1])
+    keep_own = pltpu.make_async_copy(upd.at[0], U.at[block_rows(core, z), slice_y(y)], local_sem.at[2])
+    keep_own.start()
+    load_gain = pltpu.make_async_copy(gain, GAIN16, local_sem.at[4])
+    load_gain.start()
     load_head.start()
     pl.semaphore_wait(barrier, len(peers))
-
-    own = upd.at[0]
+    keep_own.wait()
+
+    own = U.at[block_rows(core, z), slice_y(y)]
 
     def ublk(cc, zz, yy):
         return U.at[block_rows(cc, zz), slice_y(yy)]
-
-    keep_own = pltpu.make_async_copy(own, ublk(core, z, y), local_sem.at[2])
-    keep_own.start()
 
     whole = vdev // 16 * 16
 
@@ -158,7 +160,7 @@
     @pl.when(core == 1)
     def _():
         copies = []
-        order = (0, -1, 1, -2, 2, -3, 3, -4)
+        order = (0, -2, 2, -1, 1, -3, 3, -4)
 
         def send(src, dst, ssem, rsem, **device):
             copies.append(copy_to(src, dst, ssem, rsem, **device))
@@ -200,7 +202,6 @@
         return carry
 
     lax.fori_loop(0, NZ * NY, wait_sibling, 0)
-    keep_own.wait()
 
     chunk = 512
     groups = chunk // 128
@@ -225,7 +226,8 @@
     def gain_row(f, count):
         return jnp.concatenate([GAIN[pl.ds(f * count + g, 1), :] for g in range(count)], axis=1)
 
-    GAIN[...] = gain[...].astype(F32)
+    load_gain.wait()
+    GAIN[...] = GAIN16[...].astype(F32)
     lax.fori_loop(0, width // chunk, squares, 0)
     mean = jnp.sum(SQ[...], axis=1, keepdims=True) / width
     INV[...] = jnp.broadcast_to(lax.rsqrt(mean + epsilon), (rows, 128))
@@ -604,7 +606,7 @@
         copy.wait_send()
 
 
-def hand_over(upd_in, head_in, losses_in, upd_out, head_out, losses_out, upd_held, head_held, sem):
+def hand_over(upd_in, head_in, losses_in, upd_out, head_out, losses_out, upd_held, head_held, held, row, sem):
     count = 4
     step = head_in.shape[1] // count
     pairs = [(upd_in, upd_held, upd_out)]
@@ -613,13 +615,18 @@
         pairs.append((head_in.at[:, cols], head_held.at[:, cols], head_out.at[:, cols]))
     reads = [pltpu.make_async_copy(a, b, sem.at[0, n]) for n, (a, b, _) in enumerate(pairs)]
     writes = [pltpu.make_async_copy(b, c, sem.at[1, n]) for n, (_, b, c) in enumerate(pairs)]
+    read_row = pltpu.make_async_copy(losses_in, held, sem.at[0, count + 1])
+    write_row = pltpu.make_async_copy(row, losses_out, sem.at[1, count + 1])
+    read_row.start()
     for copy in reads:
         copy.start()
-    losses_out[...] = losses_in[0:1, 0:2 * NZ]
+    read_row.wait()
+    row[...] = held[0:1, 0:2 * NZ]
+    write_row.start()
     for read, write in zip(reads, writes):
         read.wait()
         write.start()
-    for copy in writes:
+    for copy in writes + [write_row]:
         copy.wait()
 
 
@@ -640,7 +647,7 @@
             jax.ShapeDtypeStruct((vdev, width // NX), BF16),
             jax.ShapeDtypeStruct((8, 128), F32),
         ),
-        in_specs=[vmem, vmem, hbm, smem, smem],
+        in_specs=[hbm, hbm, hbm, smem, smem],
         out_specs=(vmem, hbm, vmem),
         scratch_shapes=[
             pltpu.VMEM((rows, width), BF16),
@@ -657,6 +664,7 @@
             pltpu.VMEM((NX, vpad, rows), BF16),
             pltpu.VMEM((rows, vpad), BF16),
             pltpu.VMEM((vpad, rows), F32),
+            pltpu.VMEM((width // 128, 128), BF16),
             pltpu.VMEM((width // 128, 128), F32),
             pltpu.VMEM((rows, 128), F32),
             pltpu.VMEM((rows, 128), F32),
@@ -669,7 +677,7 @@
             pltpu.VMEM((2 * NY, 8, rows), F32),
             pltpu.VMEM((NZ, 8, rows), F32),
             pltpu.VMEM((NX, 8, rows), F32),
-            dma(4), dma(NZ, NY), dma(NZ, NY), dma(NZ, NY), dma(NZ, NY), dma(NZ, NY), dma(3, NZ),
+            dma(5), dma(NZ, NY), dma(NZ, NY), dma(NZ, NY), dma(NZ, NY), dma(NZ, NY), dma(3, NZ),
             dma(2 * NY + NZ), dma(2 * NY), dma(NZ), dma(2 * NY + NZ), dma(2 * NY), dma(NZ), dma(NX), dma(NX), dma(NX * 2),
             dma(NX), dma(NX), dma(NX), dma(NX), dma(NX), dma(NX), dma(NY), dma(NY), dma(slots), dma(slots),
         ],
@@ -684,9 +692,12 @@
             jax.ShapeDtypeStruct(head_grad.shape, BF16),
             jax.ShapeDtypeStruct((1, 2 * NZ), F32),
         ),
-        in_specs=[hbm, hbm, vmem],
-        out_specs=(hbm, hbm, vmem),
-        scratch_shapes=[pltpu.VMEM(upd_grad.shape, F32), pltpu.VMEM(head_grad.shape, BF16), dma(2, 5)],
+        in_specs=[hbm, hbm, hbm],
+        out_specs=(hbm, hbm, hbm),
+        scratch_shapes=[
+            pltpu.VMEM(upd_grad.shape, F32), pltpu.VMEM(head_grad.shape, BF16),
+            pltpu.VMEM((8, 128), F32), pltpu.VMEM((1, 2 * NZ), F32), dma(2, 6),
+        ],
         compiler_params=pltpu.CompilerParams(vmem_limit_bytes=60 * 1024 * 1024),
     )(upd_grad, head_grad, losses)
     return upd_grad, head_grad.T, losses.reshape(2 * NZ)

time: 85.5 us -> 83.4 us (0.975)
  Pallas kernels: 84.5 us -> 82.5 us
    pallas_call x1, Pallas kernels: 3.69 us -> 2.52 us  [body(): pl.pallas_call(hand_over, out_shape=(jax.ShapeDtypeStruct(upd_grad.shape,...]
    pallas_call x1, Pallas kernels: 80.8 us -> 79.9 us  [body(): pl.pallas_call(kernel, out_shape=(jax.ShapeDtypeStruct((1, tok, q), F32),...]
where the time goes in v1:
time: 83.4 us; the launch traced here: 83.3 us
  Pallas kernels  82.5 us (99%)
    pallas_call x1, Pallas kernels, body(): pl.pallas_call(kernel, out_shape=(jax.ShapeDtypeStruct((1, tok, q), F32),...  79.9 us
    pallas_call x1, Pallas kernels, body(): pl.pallas_call(hand_over, out_shape=(jax.ShapeDtypeStruct(upd_grad.shape,...  2.52 us

profile of v1, /device:TPU:1, one launch (start us, length us, event | category | flops | bytes accessed | tf_op | source)
XLA Modules:
  0.0 83.3 jit_solution(9257657323066651032)
XLA Ops:
  0.6 79.9 %shard_map.76 = (f32[1,16,2048]{2,1,0:T(8,128)}, bf16[500,2048]{1,0:T(8,128)(2,1)}, f32[8,128]{1,0:T(8,128)}) custom-call(bf16[1,16,2048]{2,1,0:T(8,128)(2,1)} %upd.1, bf16[64,128]{1,0:T(8,128)(2,1)} %bitcast.5, bf16[500,8192]{1,0:T(8,128)(2,1)} %bitcast.4, s32[16]{0:T(128)} %targets.1, s32[16]{0:T(128)} %curriculum.1), custom_call_target="tpu_custom_call" | custom-call | tf_op jit(solution)/shard_map/pallas_call | solution.py:643
  80.6 2.5 %shard_map.77 = (f32[1,16,2048]{2,1,0:T(8,128)}, bf16[500,2048]{1,0:T(8,128)(2,1)}, f32[1,16]{1,0:T(1,128)}) custom-call(f32[1,16,2048]{2,1,0:T(8,128)} %get-tuple-element.9.upd_in, bf16[500,2048]{1,0:T(8,128)(2,1)} %get-tuple-element.10.head_in, f32[8,128]{1,0:T(8,128)} %get-tuple-element.11.losses_in), custom_call_target="tpu_custom_call" | custom-call | tf_op jit(solution)/shard_map/pallas_call | solution.py:688
